TPU v7x, 32 devices: a whole 2x2x4 slice. The times are simulated.
32 devices in a mesh: groups: 2 (over x), col: 16 (over z, y, core).
Axes of the slice: x: 2, y: 2, z: 4, core: 2. Of those that a mesh axis runs over, the one named last changes fastest.
Arguments:
- pupils: bfloat16 [2, 32, 6144], P(None, ('groups', 'col')), parts along dimension 1, may hold values from -6 to 6
- phase_tangent: float32 [6144], replicated, may hold values from -6 to 6
- weights: float32 [32], P(('groups', 'col')), parts along dimension 0, may hold values from 0.01 to 0.1
- weight_tangent: float32 [32], P(('groups', 'col')), parts along dimension 0, may hold values from -0.3 to 0.3
- offsets: int32 [32], P(('groups', 'col')), parts along dimension 0, may hold values from 0 to 1023
- row_support: int32 [4096], P('groups'), parts along dimension 0, may hold values from 0 to 5119, as said below
- col_support: int32 [4096], replicated, may hold values from 0 to 5119, as said below
Outputs:
- tcc_tangent: float32 [2, 4096, 4096], P(None, 'groups', 'col'), parts along dimension 1
There are 2 independent parts, one for each index of `groups`. A program takes and returns all parts, laid end to end along the dimension named above; an argument that names none is the same for every part. Nothing has to cross between parts.
Inputs may be any that keep to these rules, and one draw needn't show every extreme that they name: `row_support`: distinct grid positions. `col_support`: distinct grid positions.
All inputs are finite; a program needn't handle non-finite values.
Results may differ from a plain program's by a relative error of at most 0.0034.
Values may be sent and summed in bfloat16 or wider, within the bound.
A program may use at most 128 MiB of HBM per device.

v0:
```python
import jax
import jax.numpy as jnp
from jax import lax
from jax.sharding import PartitionSpec as P


def shifted_values(pupils, offsets, support, phase_tangent):
    shifted = support[None, :] + offsets[:, None]
    real_part = jnp.take_along_axis(pupils[0], shifted, axis=1)
    imag_part = jnp.take_along_axis(pupils[1], shifted, axis=1)
    slopes = phase_tangent[shifted]
    return (real_part, imag_part, slopes)


def column_factors(real_part, imag_part, slopes, weights, weight_tangent):
    real_f = real_part.astype(jnp.float32)
    imag_f = imag_part.astype(jnp.float32)
    tangent_col = weight_tangent[:, None]
    weight_col = weights[:, None]
    x_real = (tangent_col * real_f - weight_col * slopes * imag_f).astype(jnp.bfloat16)
    x_imag = (tangent_col * imag_f + weight_col * slopes * real_f).astype(jnp.bfloat16)
    y_real = (weight_col * real_f).astype(jnp.bfloat16)
    y_imag = (weight_col * imag_f).astype(jnp.bfloat16)
    return jnp.stack([jnp.stack([x_real, y_real]), jnp.stack([x_imag, y_imag])])


def block_product(left_rows, col_block):
    width = col_block.shape[3]
    depth = 4 * col_block.shape[2]
    left_all = left_rows.reshape(depth, left_rows.shape[3])
    right_for_real = jnp.concatenate([col_block[0], col_block[1]], axis=0)
    right_for_imag = jnp.concatenate([col_block[1], -col_block[0]], axis=0)
    right_all = jnp.concatenate([right_for_real, right_for_imag], axis=2).reshape(depth, 2 * width)
    product = lax.dot_general(
        left_all, right_all, (((0,), (0,)), ((), ())), preferred_element_type=jnp.float32
    )
    return jnp.stack([product[:, :width], product[:, width:]])


def local(pupils, phase_tangent, weights, weight_tangent, offsets, row_support, col_support):
    col_real, col_imag, col_slopes = shifted_values(pupils, offsets, col_support, phase_tangent)
    columns = column_factors(col_real, col_imag, col_slopes, weights, weight_tangent)
    col_block = lax.all_to_all(columns, "col", split_axis=3, concat_axis=2, tiled=True)
    row_real, row_imag, row_slopes = shifted_values(pupils, offsets, row_support, phase_tangent)
    d_real = (-row_slopes * row_imag.astype(jnp.float32)).astype(jnp.bfloat16)
    d_imag = (row_slopes * row_real.astype(jnp.float32)).astype(jnp.bfloat16)
    rows = jnp.stack([jnp.stack([row_real, d_real]), jnp.stack([row_imag, d_imag])])
    left_rows = lax.all_gather(rows, "col", axis=2, tiled=True)
    return block_product(left_rows, col_block)


def solution(mesh):
    in_specs = (
        P(None, ("groups", "col"), None),
        P(),
        P(("groups", "col")),
        P(("groups", "col")),
        P(("groups", "col")),
        P("groups"),
        P(),
    )
    out_specs = P(None, "groups", "col")
    return jax.shard_map(local, mesh=mesh, in_specs=in_specs, out_specs=out_specs, check_vma=False)
```

profile of v0, /device:TPU:0, one launch (start us, length us, event | category | flops | bytes accessed | tf_op | source)
XLA Modules:
  0.0 171.9 jit_solution(5614788259042711962)
XLA Ops:
  0.0 0.0 copy-start
  2.0 1.0 bitcast_reduce_fusion
  2.9 0.7 fusion
  3.7 25.6 %gather_fusion.5 = bf16[4096]{0:T(1024)(128)(2,1)S(1)} fusion(bf16[6144]{0:T(1024)(128)(2,1)S(1)} %get-tuple-element.6, s32[4096]{0:T(1024)S(1)} %broadcast_clamp_fusion), kind=kCustom, calls=%fused_computation.3.clone | custom fusion | bytes 32768 | tf_op jit(solution)/shard_map/jit(take_along_axis)/gather | solution.py:10
  29.3 25.6 %gather_fusion.4 = bf16[4096]{0:T(1024)(128)(2,1)S(1)} fusion(bf16[6144]{0:T(1024)(128)(2,1)S(1)} %get-tuple-element.8, s32[4096]{0:T(1024)S(1)} %broadcast_clamp_fusion), kind=kCustom, calls=%fused_computation.1.clone | custom fusion | bytes 32768 | tf_op jit(solution)/shard_map/jit(take_along_axis)/gather | solution.py:9
  54.9 0.0 copy-done
  55.0 23.0 %gather_fusion.1 = f32[4096]{0:T(1024)S(1)} fusion(f32[6144]{0:T(1024)S(1)} %copy-done, s32[4096]{0:T(1024)S(1)} %get-tuple-element.9), kind=kCustom, calls=%fused_computation.5 | custom fusion | bytes 49152 | tf_op jit(solution)/shard_map/gather | solution.py:11
  78.0 0.1 convert_bitcast_fusion.3
  78.1 0.1 maximum_bitcast_fusion
  78.3 0.0 copy-start.2
  78.3 2.8 %copy.16 = bf16[2,2,1,4096]{1,0,2,3:T(2,128)(2,1)S(1)} copy(bf16[2,2,1,4096]{3,1,2,0:T(2,128)(2,1)S(1)} %pad_maximum_fusion.1) | data formatting | bytes 65536 | tf_op jit(solution)/shard_map/stack | solution.py:24
  81.1 3.9 %reshape.199 = bf16[16,2,512]{2,1,0:T(2,128)(2,1)} reshape(bf16[4096,1,2,2]{3,2,1,0:T(2,128)(2,1)S(1)} %bitcast.69) | data formatting | bytes 65536
  85.0 7.4 %all-to-all-start = ((bf16[16,2,512]{2,1,0:T(2,128)(2,1)}), bf16[16,2,512]{2,1,0:T(2,128)(2,1)S(1)}, u32[]{:S(2)}, u32[]{:S(2)}) async-start(bf16[16,2,512]{2,1,0:T(2,128)(2,1)} %reshape.199), calls=%async_computation | async-start | bytes 65536 | tf_op jit(solution)/shard_map/all_to_all | solution.py:43
  92.4 0.0 copy-done.2
  92.5 13.1 %gather_fusion.3 = bf16[2048]{0:T(1024)(128)(2,1)S(1)} fusion(bf16[6144]{0:T(1024)(128)(2,1)S(1)} %get-tuple-element.6, s32[2048]{0:T(1024)S(1)} %broadcast_clamp_fusion.1), kind=kCustom, calls=%fused_computation.2.clone | custom fusion | bytes 16384 | tf_op jit(solution)/shard_map/jit(take_along_axis)/gather | solution.py:10
  105.5 13.1 %gather_fusion.2 = bf16[2048]{0:T(1024)(128)(2,1)S(1)} fusion(bf16[6144]{0:T(1024)(128)(2,1)S(1)} %get-tuple-element.8, s32[2048]{0:T(1024)S(1)} %broadcast_clamp_fusion.1), kind=kCustom, calls=%fused_computation.clone | custom fusion | bytes 16384 | tf_op jit(solution)/shard_map/jit(take_along_axis)/gather | solution.py:9
  118.6 11.8 %gather_fusion = f32[2048]{0:T(1024)S(1)} fusion(f32[6144]{0:T(1024)S(1)} %copy-done, s32[2048]{0:T(1024)S(1)} %get-tuple-element.11), kind=kCustom, calls=%fused_computation.4 | custom fusion | bytes 24576 | tf_op jit(solution)/shard_map/gather | solution.py:11
  130.6 22.4 %all_gather.3 = bf16[2,2,16,2048]{3,1,2,0:T(2,128)(2,1)S(1)} all-gather(bf16[2,2,1,2048]{3,1,2,0:T(2,128)(2,1)S(1)} %pad_maximum_fusion.2), channel_id=1, replica_groups=mesh['groups'=2,'col'=16] {'col'}, dimensions={2}, use_global_device_ids=true | all-gather | bytes 278528 | tf_op jit(solution)/shard_map/all_gather | solution.py:48
  153.0 0.1 copy.15
  153.1 0.0 all-to-all-done
  153.1 4.5 %reshape.200 = bf16[4096,1,2,2]{3,2,1,0:T(2,128)(2,1)S(1)} reshape(bf16[16,2,512]{2,1,0:T(2,128)(2,1)S(1)} %all-to-all-done) | data formatting | bytes 65536
  157.7 4.2 %fusion.5 = (bf16[1,2,1,4096]{1,0,2,3:T(2,128)(2,1)}, bf16[1,2,1,4096]{1,0,2,3:T(2,128)(2,1)}) fusion(bf16[2,2,1,4096]{1,0,2,3:T(2,128)(2,1)S(1)} %bitcast.68), kind=kLoop, calls=%fused_computation.46 | loop fusion | bytes 65536 | tf_op jit(solution)/shard_map/slice | solution.py:31
  161.8 0.0 copy-start.1
  161.8 4.7 %copy.17 = bf16[1,2,1,4096]{3,1,2,0:T(2,128)(2,1)S(1)} copy(bf16[1,2,1,4096]{1,0,2,3:T(2,128)(2,1)} %get-tuple-element.16) | data formatting | bytes 32768 | tf_op jit(solution)/shard_map/slice | solution.py:31
  166.5 0.0 copy-done.1
  166.5 2.0 %copy.18 = bf16[1,2,1,4096]{3,1,2,0:T(2,128)(2,1)S(1)} copy(bf16[1,2,1,4096]{1,0,2,3:T(2,128)(2,1)S(1)} %copy-done.1) | data formatting | bytes 32768 | tf_op jit(solution)/shard_map/slice | solution.py:31
  168.5 0.7 fusion.6
  169.3 0.3 slice_bitcast_fusion.1
  169.6 2.3 %pad_maximum_fusion = f32[2,2048,256]{2,1,0:T(8,128)} fusion(f32[1,2048,256]{2,1,0:T(8,128)S(1)} %get-tuple-element.14, f32[1,2048,256]{2,1,0:T(8,128)S(1)} %get-tuple-element.13), kind=kLoop, calls=%fused_computation.6 | loop fusion | flops 1048576 | bytes 8388608 | tf_op jit(solution)/shard_map/stack | solution.py:37
  (15 shorter events, 0.3 us)
Async XLA Ops:
  0.0 54.9 %copy-start = (f32[6144]{0:T(1024)S(1)}, f32[6144]{0:T(1024)}, u32[]{:S(2)}) copy-start(f32[6144]{0:T(1024)} %param.12) | copy-start | bytes 73732
  78.3 14.1 %copy-start.2 = (s32[2048]{0:T(1024)S(1)}, s32[2048]{0:T(1024)}, u32[]{:S(2)}) copy-start(s32[2048]{0:T(1024)} %param.16) | copy-start | bytes 24580
  85.0 68.1 %all-to-all-start = ((bf16[16,2,512]{2,1,0:T(2,128)(2,1)}), bf16[16,2,512]{2,1,0:T(2,128)(2,1)S(1)}, u32[]{:S(2)}, u32[]{:S(2)}) async-start(bf16[16,2,512]{2,1,0:T(2,128)(2,1)} %reshape.199), calls=%async_computation | async-start | bytes 65536 | tf_op jit(solution)/shard_map/all_to_all | solution.py:43
  161.8 4.7 %copy-start.1 = (bf16[1,2,1,4096]{1,0,2,3:T(2,128)(2,1)S(1)}, bf16[1,2,1,4096]{1,0,2,3:T(2,128)(2,1)}, u32[]{:S(2)}) copy-start(bf16[1,2,1,4096]{1,0,2,3:T(2,128)(2,1)} %get-tuple-element.15) | copy-start | bytes 49156
where the time goes:
time: 172 us
  local copies, waits for them, and re-layouts  136 us (79%)
  blocking collectives  22.4 us (13%)
  starting transfers between devices  7.39 us (4%)
  other arithmetic  3.44 us (2%)
  between operations  2.22 us (1%)
    gather x2, local copies, waits for them, and re-layouts, shifted_values(): imag_part = jnp.take_along_axis(pupils[1], shifted, axis=1)  38.7 us
    gather x2, local copies, waits for them, and re-layouts, shifted_values(): real_part = jnp.take_along_axis(pupils[0], shifted, axis=1)  38.7 us
    gather x2, local copies, waits for them, and re-layouts, shifted_values(): slopes = phase_tangent[shifted]  34.8 us
    all_gather x1, blocking collectives, local(): left_rows = lax.all_gather(rows, 'col', axis=2, tiled=True)  22.4 us
    slice x3, local copies, waits for them, and re-layouts, block_product(): right_for_real = jnp.concatenate([col_block[0], col_block[1]], axis=0)  10.8 us
    unnamed x10, local copies, waits for them, and re-layouts  8.51 us
    all_to_all x1, starting transfers between devices, local(): lax.all_to_all(columns, 'col', split_axis=3, concat_axis=2, tiled=True)  7.39 us
  transfers between devices with their start and end apart: 1, of which 0 were waited for; matrix products, arithmetic and copies ran while one was open for 22% of the time, Pallas kernels for 0%

commit v1 on v0

--- a/solution.py
+++ b/solution.py
@@ -1,7 +1,17 @@
+import functools
+
 import jax
 import jax.numpy as jnp
 from jax import lax
+from jax.experimental import pallas as pl
+from jax.experimental.pallas import tpu as pltpu
 from jax.sharding import PartitionSpec as P
+
+LANES = 128
+SCALAR_ROWS = 16
+PARTS = 8
+TABLE_LIMIT_BYTES = 8 * 1024 * 1024
+MESH = pl.DeviceIdType.MESH
 
 
 def shifted_values(pupils, offsets, support, phase_tangent):
@@ -37,7 +47,7 @@
     return jnp.stack([product[:, :width], product[:, width:]])
 
 
-def local(pupils, phase_tangent, weights, weight_tangent, offsets, row_support, col_support):
+def exchanged(pupils, phase_tangent, weights, weight_tangent, offsets, row_support, col_support):
     col_real, col_imag, col_slopes = shifted_values(pupils, offsets, col_support, phase_tangent)
     columns = column_factors(col_real, col_imag, col_slopes, weights, weight_tangent)
     col_block = lax.all_to_all(columns, "col", split_axis=3, concat_axis=2, tiled=True)
@@ -49,6 +59,212 @@
     return block_product(left_rows, col_block)
 
 
+def split3(value):
+    high = value.astype(jnp.bfloat16).astype(jnp.float32)
+    rest = value - high
+    middle = rest.astype(jnp.bfloat16).astype(jnp.float32)
+    return high, middle, rest - middle
+
+
+def gather_kernel(n, chunks, pupil_ref, w_ref, wt_ref, off_ref, out_ref, wide, packed, send_sem, recv_sem, own_sem):
+    me = lax.axis_index("col")
+    barrier = pltpu.get_barrier_semaphore()
+    for k in range(1, n):
+        pl.semaphore_signal(barrier, inc=1, device_id={"col": lax.rem(me + k, n)}, device_id_type=MESH)
+
+    values = pupil_ref[...].astype(jnp.float32)
+    for part in range(2):
+        for chunk in range(chunks):
+            row = part * chunks + chunk
+            wide[row : row + 1, :] = values[part : part + 1, chunk * LANES : (chunk + 1) * LANES]
+    lane = lax.broadcasted_iota(jnp.int32, (SCALAR_ROWS, LANES), 1)
+    scalars = jnp.zeros((SCALAR_ROWS, LANES), jnp.float32)
+    place = 0
+    for scalar in (w_ref[0], wt_ref[0], off_ref[0].astype(jnp.float32)):
+        for piece in split3(jnp.full((SCALAR_ROWS, LANES), scalar, jnp.float32)):
+            scalars = jnp.where(lane == place, piece, scalars)
+            place += 1
+    wide[2 * chunks :, :] = scalars
+    packed[...] = wide[...].astype(jnp.bfloat16)
+
+    own = pltpu.make_async_copy(packed, out_ref.at[me], own_sem)
+    own.start()
+    pl.semaphore_wait(barrier, n - 1)
+    copies = []
+    for k in range(1, n):
+        copy = pltpu.make_async_remote_copy(
+            src_ref=packed,
+            dst_ref=out_ref.at[me],
+            send_sem=send_sem.at[k - 1],
+            recv_sem=recv_sem.at[k - 1],
+            device_id={"col": lax.rem(me + k, n)},
+            device_id_type=MESH,
+        )
+        copy.start()
+        copies.append(copy)
+    own.wait()
+    for copy in copies:
+        copy.wait()
+
+
+def gathered_pupils(n, pupils, weights, weight_tangent, offsets):
+    grid_size = pupils.shape[2]
+    chunks = grid_size // LANES
+    rows = 2 * chunks + SCALAR_ROWS
+    smem = pl.BlockSpec(memory_space=pltpu.SMEM)
+    return pl.pallas_call(
+        functools.partial(gather_kernel, n, chunks),
+        out_shape=jax.ShapeDtypeStruct((n, rows, LANES), jnp.bfloat16),
+        in_specs=[pl.BlockSpec(memory_space=pltpu.VMEM), smem, smem, smem],
+        out_specs=pl.BlockSpec(memory_space=pl.ANY),
+        scratch_shapes=[
+            pltpu.VMEM((rows, LANES), jnp.float32),
+            pltpu.VMEM((rows, LANES), jnp.bfloat16),
+            pltpu.SemaphoreType.DMA((n - 1,)),
+            pltpu.SemaphoreType.DMA((n - 1,)),
+            pltpu.SemaphoreType.DMA,
+        ],
+        compiler_params=pltpu.CompilerParams(collective_id=0, has_side_effects=True),
+        name="gather_pupils",
+    )(pupils.reshape(2, grid_size), weights, weight_tangent, offsets)
+
+
+def rounded(value):
+    return value.astype(jnp.bfloat16).astype(jnp.float32)
+
+
+def shift_rows(source, start, reach, lane_shift, lane):
+    lower = source[pl.ds(start, reach), :]
+    upper = source[pl.ds(start + 1, reach), :]
+    return pltpu.roll(jnp.where(lane >= lane_shift, lower, upper), lax.rem(LANES - lane_shift, LANES), 1)
+
+
+def block_kernel(
+    sources, chunks, reach, tile, width,
+    offset_ref, row_ref, col_ref, all_ref, phase_ref, out_ref,
+    wide, shifted, factors, table, picked, right,
+):
+    depth = 4 * sources
+
+    def pick(index_ref, base, count):
+        def eight(group, carry):
+            first = pl.multiple_of(group * 8, 8)
+            for k in range(8):
+                picked[pl.ds(first + k, 1), :] = table[pl.ds(index_ref[base + first + k], 1), :]
+            return carry
+
+        lax.fori_loop(0, count // 8, eight, 0, unroll=4)
+
+    @pl.when(pl.program_id(0) == 0)
+    def _():
+        lane = lax.broadcasted_iota(jnp.int32, (reach, LANES), 1)
+        for s in range(sources):
+            wide[...] = all_ref[s, : 2 * chunks, :].astype(jnp.float32)
+            scalars = all_ref[s, 2 * chunks : 2 * chunks + SCALAR_ROWS, :].astype(jnp.float32)[:1, :]
+            factors[s : s + 1, :] = jnp.broadcast_to(
+                scalars[:, 0:1] + scalars[:, 1:2] + scalars[:, 2:3], (1, LANES)
+            )
+            factors[sources + s : sources + s + 1, :] = jnp.broadcast_to(
+                scalars[:, 3:4] + scalars[:, 4:5] + scalars[:, 5:6], (1, LANES)
+            )
+            offset = offset_ref[s]
+            start = offset // LANES
+            lane_shift = lax.rem(offset, LANES)
+            spread = pl.ds(s, reach, stride=sources)
+            shifted[0, spread, :] = shift_rows(wide, start, reach, lane_shift, lane)
+            shifted[1, spread, :] = shift_rows(wide, chunks + start, reach, lane_shift, lane)
+            shifted[2, spread, :] = shift_rows(phase_ref, start, reach, lane_shift, lane)
+        weight = factors[:sources, :]
+        tangent = factors[sources:, :]
+
+        def one_chunk(chunk, carry):
+            at = pl.ds(pl.multiple_of(chunk * sources, sources), sources)
+            real, imag, slope = shifted[0, at, :], shifted[1, at, :], shifted[2, at, :]
+            tilted = weight * slope
+            block = jnp.concatenate(
+                [
+                    real,
+                    -slope * imag,
+                    imag,
+                    slope * real,
+                    tangent * real - tilted * imag,
+                    weight * real,
+                    tangent * imag + tilted * real,
+                    weight * imag,
+                ],
+                axis=0,
+            )
+            table[pl.ds(pl.multiple_of(chunk * LANES, LANES), LANES), :] = rounded(block).T
+            return carry
+
+        lax.fori_loop(0, reach, one_chunk, 0, unroll=2)
+
+        pick(col_ref, 0, width)
+        columns = pltpu.roll(picked[:width, :], PARTS * sources - depth, 1)
+        column_lane = lax.broadcasted_iota(jnp.int32, (width, LANES), 1)
+        swapped = pltpu.roll(columns, LANES - depth // 2, 1)
+        crossed = pltpu.roll(columns, depth // 2, 1)
+        zero = jnp.zeros_like(columns)
+        right[:width, :] = jnp.where(column_lane < depth, columns, zero).astype(jnp.bfloat16)
+        right[width:, :] = jnp.where(
+            column_lane < depth // 2, swapped, jnp.where(column_lane < depth, -crossed, zero)
+        ).astype(jnp.bfloat16)
+
+    pick(row_ref, pl.program_id(0) * tile, tile)
+    product = lax.dot_general(
+        picked[:tile, :].astype(jnp.bfloat16), right[...], (((1,), (1,)), ((), ())),
+        preferred_element_type=jnp.float32,
+    )
+    out_ref[0] = product[:, :width]
+    out_ref[1] = product[:, width:]
+
+
+def block_row(sources, reach, everything, offsets, phase_tangent, row_support, col_here):
+    chunks = phase_tangent.shape[0] // LANES
+    rows, width = row_support.shape[0], col_here.shape[0]
+    tile = 256
+    whole = pl.BlockSpec(memory_space=pltpu.VMEM)
+    smem = pl.BlockSpec(memory_space=pltpu.SMEM)
+    return pl.pallas_call(
+        functools.partial(block_kernel, sources, chunks, reach, tile, width),
+        out_shape=jax.ShapeDtypeStruct((2, rows, width), jnp.float32),
+        grid=(rows // tile,),
+        in_specs=[smem, smem, smem, whole, whole],
+        out_specs=pl.BlockSpec((2, tile, width), lambda i: (0, i, 0)),
+        scratch_shapes=[
+            pltpu.VMEM((2 * chunks, LANES), jnp.float32),
+            pltpu.VMEM((3, reach * sources, LANES), jnp.float32),
+            pltpu.VMEM((2 * sources, LANES), jnp.float32),
+            pltpu.VMEM((reach * LANES, LANES), jnp.float32),
+            pltpu.VMEM((max(tile, width), LANES), jnp.float32),
+            pltpu.VMEM((2 * width, LANES), jnp.bfloat16),
+        ],
+        compiler_params=pltpu.CompilerParams(vmem_limit_bytes=32 * 1024 * 1024),
+        name="block_row",
+    )(offsets, row_support, col_here, everything, phase_tangent.reshape(chunks, LANES))
+
+
+def local(n, pupils, phase_tangent, weights, weight_tangent, offsets, row_support, col_support):
+    grid_size = phase_tangent.shape[0]
+    rows = row_support.shape[0]
+    width = col_support.shape[0] // n
+    reach = grid_size // 6 * 5 // LANES
+    fits = (
+        PARTS * n == LANES
+        and grid_size % (6 * LANES) == 0
+        and rows % 256 == 0
+        and width % LANES == 0
+        and grid_size * LANES * 4 <= TABLE_LIMIT_BYTES
+    )
+    if not fits:
+        return exchanged(pupils, phase_tangent, weights, weight_tangent, offsets, row_support, col_support)
+    everything = gathered_pupils(n, pupils, weights, weight_tangent, offsets)
+    start = 2 * (grid_size // LANES)
+    all_offsets = everything[:, start, 6:9].astype(jnp.float32).sum(axis=1).astype(jnp.int32)
+    col_here = lax.dynamic_slice(col_support, (lax.axis_index("col") * width,), (width,))
+    return block_row(n, reach, everything, all_offsets, phase_tangent, row_support, col_here)
+
+
 def solution(mesh):
     in_specs = (
         P(None, ("groups", "col"), None),
@@ -60,4 +276,7 @@
         P(),
     )
     out_specs = P(None, "groups", "col")
-    return jax.shard_map(local, mesh=mesh, in_specs=in_specs, out_specs=out_specs, check_vma=False)
+    return jax.shard_map(
+        functools.partial(local, mesh.shape["col"]),
+        mesh=mesh, in_specs=in_specs, out_specs=out_specs, check_vma=False,
+    )

time: 172 us -> 32.4 us (0.19)
  the two profiles are of different devices: /device:TPU:0 before, /device:TPU:13 now
where the time goes in v1:
time: 32.4 us; the launch traced here: 32 us
  Pallas kernels  25.7 us (79%)
  local copies, waits for them, and re-layouts  3.22 us (10%)
  between operations  1.96 us (6%)
  other arithmetic  1.05 us (3%)
    pallas_call x1, Pallas kernels, gathered_pupils(): pl.pallas_call(functools.partial(gather_kernel, n, chunks), out_shape=jax...  16 us
    pallas_call x1, Pallas kernels, block_row(): pl.pallas_call(functools.partial(block_kernel, sources, chunks, reach, ti...  9.71 us
    unnamed x6, local copies, waits for them, and re-layouts  2.46 us
    reduce_sum x1, other arithmetic, local(): everything[:, start, 6:9].astype(jnp.float32).sum(axis=1).astype(jnp.int32)  1.05 us
    dynamic_slice x1, local copies, waits for them, and re-layouts, local(): lax.dynamic_slice(col_support, (lax.axis_index('col') * width,), (width,))  0.76 us

profile of v1, /device:TPU:13, one launch (start us, length us, event | category | flops | bytes accessed | tf_op | source)
XLA Modules:
  0.0 32.0 jit_solution(12784237692111127654)
XLA Ops:
  1.9 0.8 %dynamic_slice.3.col_ref = s32[256]{0:T(256)S(1)} dynamic-slice(s32[4096]{0:T(1024)} %param.13, s32[]{:T(128)S(6)} %select_n.3), dynamic_slice_sizes={256} | dynamic-slice | bytes 2052 | tf_op jit(solution)/shard_map/dynamic_slice | solution.py:264
  2.7 16.0 %gather_pupils.1.all_ref = bf16[16,112,128]{2,1,0:T(8,128)(2,1)} custom-call(bf16[2,6144]{1,0:T(2,128)(2,1)} %bitcast.3, f32[1]{0:T(128)S(6)} %copy.8.w_ref, f32[1]{0:T(128)S(6)} %copy.9.wt_ref, s32[1]{0:T(128)S(6)} %copy.10.off_ref), custom_call_target="tpu_custom_call" | custom-call | tf_op jit(solution)/shard_map/gather_pupils/pallas_call | solution.py:115
  18.7 1.0 %convert_reduce_fusion = f32[16]{0:T(128)S(1)} fusion(bf16[16,112,128]{2,1,0:T(8,128)(2,1)} %gather_pupils.1.all_ref), kind=kLoop, calls=%fused_computation | loop fusion | flops 80 | bytes 160 | tf_op jit(solution)/shard_map/reduce_sum | solution.py:263
  19.8 0.0 copy-start
  19.8 1.0 %copy-done = bf16[16,112,128]{2,1,0:T(8,128)(2,1)S(1)} copy-done((bf16[16,112,128]{2,1,0:T(8,128)(2,1)S(1)}, bf16[16,112,128]{2,1,0:T(8,128)(2,1)}, u32[]{:S(2)}) %copy-start) | copy-done | bytes 458776
  20.8 0.0 copy-start.1
  20.8 0.7 %copy-done.1 = f32[6144]{0:T(1024)S(1)} copy-done((f32[6144]{0:T(1024)S(1)}, f32[6144]{0:T(1024)}, u32[]{:S(2)}) %copy-start.1) | copy-done | bytes 24600
  21.6 0.0 copy-start.2
  21.6 0.7 %copy-done.2 = s32[2048]{0:T(1024)S(1)} copy-done((s32[2048]{0:T(1024)S(1)}, s32[2048]{0:T(1024)}, u32[]{:S(2)}) %copy-start.2) | copy-done | bytes 8216
  22.3 9.7 %block_row.1 = f32[2,2048,256]{2,1,0:T(8,128)} custom-call(s32[16]{0:T(128)S(1)} %convert_element_type.8.offset_ref, s32[2048]{0:T(1024)S(1)} %copy-done.2, s32[256]{0:T(256)S(1)} %dynamic_slice.3.col_ref, bf16[16,112,128]{2,1,0:T(8,128)(2,1)S(1)} %copy-done, f32[48,128]{1,0:T(8,128)S(1)} %bitcast.2), custom_call_target="tpu_custom_call" | custom-call | tf_op jit(solution)/shard_map/block_row/pallas_call | solution.py:228
  (1 shorter events, 0.0 us)
Async XLA Ops:
  19.8 1.0 %copy-start = (bf16[16,112,128]{2,1,0:T(8,128)(2,1)S(1)}, bf16[16,112,128]{2,1,0:T(8,128)(2,1)}, u32[]{:S(2)}) copy-start(bf16[16,112,128]{2,1,0:T(8,128)(2,1)} %gather_pupils.1.all_ref) | copy-start | bytes 1376260
  20.8 0.7 %copy-start.1 = (f32[6144]{0:T(1024)S(1)}, f32[6144]{0:T(1024)}, u32[]{:S(2)}) copy-start(f32[6144]{0:T(1024)} %param.8) | copy-start | bytes 73732
  21.6 0.7 %copy-start.2 = (s32[2048]{0:T(1024)S(1)}, s32[2048]{0:T(1024)}, u32[]{:S(2)}) copy-start(s32[2048]{0:T(1024)} %row_ref.1) | copy-start | bytes 24580

commit v2 on v1

--- a/solution.py
+++ b/solution.py
@@ -10,6 +10,7 @@
 LANES = 128
 SCALAR_ROWS = 16
 PARTS = 8
+PICKS = 32
 TABLE_LIMIT_BYTES = 8 * 1024 * 1024
 MESH = pl.DeviceIdType.MESH
 
@@ -66,12 +67,29 @@
     return high, middle, rest - middle
 
 
-def gather_kernel(n, chunks, pupil_ref, w_ref, wt_ref, off_ref, out_ref, wide, packed, send_sem, recv_sem, own_sem):
+def gather_kernel(
+    n, chunks, pupil_hbm, w_ref, wt_ref, off_ref, out_ref, pupil_ref, wide, packed, send_sem, recv_sem, own_sem
+):
+    load = pltpu.make_async_copy(pupil_hbm, pupil_ref, own_sem)
+    load.start()
     me = lax.axis_index("col")
+    quarter = n // 4
+    core = lax.rem(me, 2)
+    far = quarter * (me // quarter)
+    near = lax.rem(me, quarter)
+    sibling = far + near + 1 - 2 * core
+    across_near = lax.rem(near + quarter // 2, quarter)
+    across = far + across_near
+
+    def ahead(k):
+        return lax.rem(me + k * quarter, n)
+
     barrier = pltpu.get_barrier_semaphore()
-    for k in range(1, n):
-        pl.semaphore_signal(barrier, inc=1, device_id={"col": lax.rem(me + k, n)}, device_id_type=MESH)
-
+    partners = [ahead(1), ahead(2), ahead(3), across, sibling]
+    for partner in partners:
+        pl.semaphore_signal(barrier, inc=1, device_id={"col": partner}, device_id_type=MESH)
+
+    load.wait()
     values = pupil_ref[...].astype(jnp.float32)
     for part in range(2):
         for chunk in range(chunks):
@@ -89,22 +107,37 @@
 
     own = pltpu.make_async_copy(packed, out_ref.at[me], own_sem)
     own.start()
-    pl.semaphore_wait(barrier, n - 1)
-    copies = []
-    for k in range(1, n):
+    pl.semaphore_wait(barrier, len(partners))
+
+    def send(source, slot, index, partner):
         copy = pltpu.make_async_remote_copy(
-            src_ref=packed,
-            dst_ref=out_ref.at[me],
-            send_sem=send_sem.at[k - 1],
-            recv_sem=recv_sem.at[k - 1],
-            device_id={"col": lax.rem(me + k, n)},
+            src_ref=source,
+            dst_ref=out_ref.at[slot],
+            send_sem=send_sem.at[index],
+            recv_sem=recv_sem.at[index],
+            device_id={"col": partner},
             device_id_type=MESH,
         )
         copy.start()
-        copies.append(copy)
+        return copy
+
+    copies = {k: send(packed, me, k, ahead(k)) for k in (2, 1, 3)}
+    copies[4] = send(packed, me, 4, across)
+    copies[8] = send(packed, me, 8, sibling)
+    for k in (1, 3, 2):
+        copies[k].wait_recv()
+        slot = lax.rem(me + (4 - k) * quarter, n)
+        copies[4 + k] = send(out_ref.at[slot], slot, 4 + k, across)
+        copies[8 + k] = send(out_ref.at[slot], slot, 8 + k, sibling)
+    for k in (0, 1, 3, 2):
+        copies[4 + k].wait_recv()
+        slot = lax.rem(far + (4 - k) * quarter, n) + across_near
+        copies[12 + k] = send(out_ref.at[slot], slot, 12 + k, sibling)
     own.wait()
-    for copy in copies:
-        copy.wait()
+    for k in range(8):
+        copies[8 + k].wait_recv()
+    for k in range(1, 16):
+        copies[k].wait_send()
 
 
 def gathered_pupils(n, pupils, weights, weight_tangent, offsets):
@@ -115,13 +148,14 @@
     return pl.pallas_call(
         functools.partial(gather_kernel, n, chunks),
         out_shape=jax.ShapeDtypeStruct((n, rows, LANES), jnp.bfloat16),
-        in_specs=[pl.BlockSpec(memory_space=pltpu.VMEM), smem, smem, smem],
-        out_specs=pl.BlockSpec(memory_space=pl.ANY),
+        in_specs=[pl.BlockSpec(memory_space=pltpu.HBM), smem, smem, smem],
+        out_specs=pl.BlockSpec(memory_space=pltpu.HBM),
         scratch_shapes=[
+            pltpu.VMEM((2, grid_size), jnp.bfloat16),
             pltpu.VMEM((rows, LANES), jnp.float32),
             pltpu.VMEM((rows, LANES), jnp.bfloat16),
-            pltpu.SemaphoreType.DMA((n - 1,)),
-            pltpu.SemaphoreType.DMA((n - 1,)),
+            pltpu.SemaphoreType.DMA((16,)),
+            pltpu.SemaphoreType.DMA((16,)),
             pltpu.SemaphoreType.DMA,
         ],
         compiler_params=pltpu.CompilerParams(collective_id=0, has_side_effects=True),
@@ -141,39 +175,51 @@
 
 def block_kernel(
     sources, chunks, reach, tile, width,
-    offset_ref, row_ref, col_ref, all_ref, phase_ref, out_ref,
-    wide, shifted, factors, table, picked, right,
+    row_hbm, col_hbm, all_hbm, phase_hbm, out_ref,
+    rows, cols, everything, phase, wide, shifted, factors, table, picked, right, sems,
 ):
     depth = 4 * sources
 
     def pick(index_ref, base, count):
-        def eight(group, carry):
-            first = pl.multiple_of(group * 8, 8)
-            for k in range(8):
+        def some(group, carry):
+            first = pl.multiple_of(group * PICKS, 8)
+            for k in range(PICKS):
                 picked[pl.ds(first + k, 1), :] = table[pl.ds(index_ref[base + first + k], 1), :]
             return carry
 
-        lax.fori_loop(0, count // 8, eight, 0, unroll=4)
+        lax.fori_loop(0, count // PICKS, some, 0)
 
     @pl.when(pl.program_id(0) == 0)
     def _():
+        copies = [
+            pltpu.make_async_copy(source, target, sems.at[i])
+            for i, (source, target) in enumerate(
+                [(all_hbm, everything), (phase_hbm, phase), (row_hbm, rows), (col_hbm, cols)]
+            )
+        ]
+        for copy in copies:
+            copy.start()
+        copies[0].wait()
+        copies[1].wait()
         lane = lax.broadcasted_iota(jnp.int32, (reach, LANES), 1)
+        offsets = []
         for s in range(sources):
-            wide[...] = all_ref[s, : 2 * chunks, :].astype(jnp.float32)
-            scalars = all_ref[s, 2 * chunks : 2 * chunks + SCALAR_ROWS, :].astype(jnp.float32)[:1, :]
-            factors[s : s + 1, :] = jnp.broadcast_to(
-                scalars[:, 0:1] + scalars[:, 1:2] + scalars[:, 2:3], (1, LANES)
+            scalars = everything[s, 2 * chunks : 2 * chunks + SCALAR_ROWS, :].astype(jnp.float32)[:1, :]
+            one, two, three = (
+                scalars[:, i : i + 1] + scalars[:, i + 1 : i + 2] + scalars[:, i + 2 : i + 3] for i in (0, 3, 6)
             )
-            factors[sources + s : sources + s + 1, :] = jnp.broadcast_to(
-                scalars[:, 3:4] + scalars[:, 4:5] + scalars[:, 5:6], (1, LANES)
-            )
-            offset = offset_ref[s]
-            start = offset // LANES
-            lane_shift = lax.rem(offset, LANES)
+            factors[s : s + 1, :] = jnp.broadcast_to(one, (1, LANES))
+            factors[sources + s : sources + s + 1, :] = jnp.broadcast_to(two, (1, LANES))
+            offsets.append(three[0, 0].astype(jnp.int32))
+        for s in range(sources):
+            own = wide.at[s % 2]
+            own[...] = everything[s, : 2 * chunks, :].astype(jnp.float32)
+            start = offsets[s] // LANES
+            lane_shift = lax.rem(offsets[s], LANES)
             spread = pl.ds(s, reach, stride=sources)
-            shifted[0, spread, :] = shift_rows(wide, start, reach, lane_shift, lane)
-            shifted[1, spread, :] = shift_rows(wide, chunks + start, reach, lane_shift, lane)
-            shifted[2, spread, :] = shift_rows(phase_ref, start, reach, lane_shift, lane)
+            shifted[0, spread, :] = shift_rows(own, start, reach, lane_shift, lane)
+            shifted[1, spread, :] = shift_rows(own, chunks + start, reach, lane_shift, lane)
+            shifted[2, spread, :] = shift_rows(phase, start, reach, lane_shift, lane)
         weight = factors[:sources, :]
         tangent = factors[sources:, :]
 
@@ -199,7 +245,9 @@
 
         lax.fori_loop(0, reach, one_chunk, 0, unroll=2)
 
-        pick(col_ref, 0, width)
+        copies[2].wait()
+        copies[3].wait()
+        pick(cols, lax.axis_index("col") * width, width)
         columns = pltpu.roll(picked[:width, :], PARTS * sources - depth, 1)
         column_lane = lax.broadcasted_iota(jnp.int32, (width, LANES), 1)
         swapped = pltpu.roll(columns, LANES - depth // 2, 1)
@@ -210,7 +258,7 @@
             column_lane < depth // 2, swapped, jnp.where(column_lane < depth, -crossed, zero)
         ).astype(jnp.bfloat16)
 
-    pick(row_ref, pl.program_id(0) * tile, tile)
+    pick(rows, pl.program_id(0) * tile, tile)
     product = lax.dot_general(
         picked[:tile, :].astype(jnp.bfloat16), right[...], (((1,), (1,)), ((), ())),
         preferred_element_type=jnp.float32,
@@ -219,29 +267,32 @@
     out_ref[1] = product[:, width:]
 
 
-def block_row(sources, reach, everything, offsets, phase_tangent, row_support, col_here):
+def block_row(sources, reach, everything, phase_tangent, row_support, col_support):
     chunks = phase_tangent.shape[0] // LANES
-    rows, width = row_support.shape[0], col_here.shape[0]
+    rows, width = row_support.shape[0], col_support.shape[0] // sources
     tile = 256
-    whole = pl.BlockSpec(memory_space=pltpu.VMEM)
-    smem = pl.BlockSpec(memory_space=pltpu.SMEM)
     return pl.pallas_call(
         functools.partial(block_kernel, sources, chunks, reach, tile, width),
         out_shape=jax.ShapeDtypeStruct((2, rows, width), jnp.float32),
         grid=(rows // tile,),
-        in_specs=[smem, smem, smem, whole, whole],
+        in_specs=[pl.BlockSpec(memory_space=pltpu.HBM)] * 4,
         out_specs=pl.BlockSpec((2, tile, width), lambda i: (0, i, 0)),
         scratch_shapes=[
-            pltpu.VMEM((2 * chunks, LANES), jnp.float32),
+            pltpu.SMEM(row_support.shape, jnp.int32),
+            pltpu.SMEM(col_support.shape, jnp.int32),
+            pltpu.VMEM(everything.shape, jnp.bfloat16),
+            pltpu.VMEM((chunks, LANES), jnp.float32),
+            pltpu.VMEM((2, 2 * chunks, LANES), jnp.float32),
             pltpu.VMEM((3, reach * sources, LANES), jnp.float32),
             pltpu.VMEM((2 * sources, LANES), jnp.float32),
             pltpu.VMEM((reach * LANES, LANES), jnp.float32),
             pltpu.VMEM((max(tile, width), LANES), jnp.float32),
             pltpu.VMEM((2 * width, LANES), jnp.bfloat16),
+            pltpu.SemaphoreType.DMA((4,)),
         ],
-        compiler_params=pltpu.CompilerParams(vmem_limit_bytes=32 * 1024 * 1024),
+        compiler_params=pltpu.CompilerParams(vmem_limit_bytes=48 * 1024 * 1024),
         name="block_row",
-    )(offsets, row_support, col_here, everything, phase_tangent.reshape(chunks, LANES))
+    )(row_support, col_support, everything, phase_tangent.reshape(chunks, LANES))
 
 
 def local(n, pupils, phase_tangent, weights, weight_tangent, offsets, row_support, col_support):
@@ -259,10 +310,7 @@
     if not fits:
         return exchanged(pupils, phase_tangent, weights, weight_tangent, offsets, row_support, col_support)
     everything = gathered_pupils(n, pupils, weights, weight_tangent, offsets)
-    start = 2 * (grid_size // LANES)
-    all_offsets = everything[:, start, 6:9].astype(jnp.float32).sum(axis=1).astype(jnp.int32)
-    col_here = lax.dynamic_slice(col_support, (lax.axis_index("col") * width,), (width,))
-    return block_row(n, reach, everything, all_offsets, phase_tangent, row_support, col_here)
+    return block_row(n, reach, everything, phase_tangent, row_support, col_support)
 
 
 def solution(mesh):

time: 32.4 us -> 28.7 us (0.89)
  the two profiles are of different devices: /device:TPU:13 before, /device:TPU:0 now
where the time goes in v2:
time: 28.7 us; the launch traced here: 28.3 us
  Pallas kernels  23.1 us (80%)
  local copies, waits for them, and re-layouts  3.16 us (11%)
  between operations  1.96 us (7%)
    pallas_call x1, Pallas kernels, gathered_pupils(): pl.pallas_call(functools.partial(gather_kernel, n, chunks), out_shape=jax...  14 us
    pallas_call x1, Pallas kernels, block_row(): pl.pallas_call(functools.partial(block_kernel, sources, chunks, reach, ti...  9.18 us
    unnamed x8, local copies, waits for them, and re-layouts  3.16 us

profile of v2, /device:TPU:0, one launch (start us, length us, event | category | flops | bytes accessed | tf_op | source)
XLA Modules:
  0.0 28.3 jit_solution(14081872897846248288)
XLA Ops:
  1.9 14.0 %gather_pupils.1.all_hbm = bf16[16,112,128]{2,1,0:T(8,128)(2,1)} custom-call(bf16[2,6144]{1,0:T(2,128)(2,1)} %bitcast.3, f32[1]{0:T(128)S(6)} %copy.8.w_ref, f32[1]{0:T(128)S(6)} %copy.9.wt_ref, s32[1]{0:T(128)S(6)} %copy.10.off_ref), custom_call_target="tpu_custom_call" | custom-call | tf_op jit(solution)/shard_map/gather_pupils/pallas_call | solution.py:148
  15.9 0.0 copy-start
  15.9 1.0 %copy-done = bf16[16,112,128]{2,1,0:T(8,128)(2,1)S(1)} copy-done((bf16[16,112,128]{2,1,0:T(8,128)(2,1)S(1)}, bf16[16,112,128]{2,1,0:T(8,128)(2,1)}, u32[]{:S(2)}) %copy-start) | copy-done | bytes 458776
  16.9 0.0 copy-start.1
  16.9 0.7 %copy-done.1 = f32[6144]{0:T(1024)S(1)} copy-done((f32[6144]{0:T(1024)S(1)}, f32[6144]{0:T(1024)}, u32[]{:S(2)}) %copy-start.1) | copy-done | bytes 24600
  17.7 0.0 copy-start.2
  17.7 0.7 %copy-done.2 = s32[4096]{0:T(1024)S(1)} copy-done((s32[4096]{0:T(1024)S(1)}, s32[4096]{0:T(1024)}, u32[]{:S(2)}) %copy-start.2) | copy-done | bytes 16408
  18.4 0.0 copy-start.3
  18.4 0.7 %copy-done.3 = s32[2048]{0:T(1024)S(1)} copy-done((s32[2048]{0:T(1024)S(1)}, s32[2048]{0:T(1024)}, u32[]{:S(2)}) %copy-start.3) | copy-done | bytes 8216
  19.1 9.2 %block_row.1 = f32[2,2048,256]{2,1,0:T(8,128)} custom-call(s32[2048]{0:T(1024)S(1)} %copy-done.3, s32[4096]{0:T(1024)S(1)} %copy-done.2, bf16[16,112,128]{2,1,0:T(8,128)(2,1)S(1)} %copy-done, f32[48,128]{1,0:T(8,128)S(1)} %bitcast.2), custom_call_target="tpu_custom_call" | custom-call | tf_op jit(solution)/shard_map/block_row/pallas_call | solution.py:274
Async XLA Ops:
  15.9 1.0 %copy-start = (bf16[16,112,128]{2,1,0:T(8,128)(2,1)S(1)}, bf16[16,112,128]{2,1,0:T(8,128)(2,1)}, u32[]{:S(2)}) copy-start(bf16[16,112,128]{2,1,0:T(8,128)(2,1)} %gather_pupils.1.all_hbm) | copy-start | bytes 1376260
  16.9 0.7 %copy-start.1 = (f32[6144]{0:T(1024)S(1)}, f32[6144]{0:T(1024)}, u32[]{:S(2)}) copy-start(f32[6144]{0:T(1024)} %param.8) | copy-start | bytes 73732
  17.7 0.7 %copy-start.2 = (s32[4096]{0:T(1024)S(1)}, s32[4096]{0:T(1024)}, u32[]{:S(2)}) copy-start(s32[4096]{0:T(1024)} %col_hbm.1) | copy-start | bytes 49156
  18.4 0.7 %copy-start.3 = (s32[2048]{0:T(1024)S(1)}, s32[2048]{0:T(1024)}, u32[]{:S(2)}) copy-start(s32[2048]{0:T(1024)} %row_hbm.1) | copy-start | bytes 24580

commit v3 on v2

--- a/solution.py
+++ b/solution.py
@@ -8,9 +8,10 @@
 from jax.sharding import PartitionSpec as P
 
 LANES = 128
-SCALAR_ROWS = 16
 PARTS = 8
-PICKS = 32
+PICKS = 64
+TILE = 512
+ORDER = (1, 7, 2, 6, 3, 5, 4)
 TABLE_LIMIT_BYTES = 8 * 1024 * 1024
 MESH = pl.DeviceIdType.MESH
 
@@ -67,47 +68,60 @@
     return high, middle, rest - middle
 
 
+def half_rows(reach):
+    return (reach + 16) // 16 * 16
+
+
+def shift_rows(source, start, reach, lane_shift, lane):
+    lower = source[pl.ds(start, reach), :]
+    upper = source[pl.ds(start + 1, reach), :]
+    return pltpu.roll(jnp.where(lane >= lane_shift, lower, upper), (LANES - lane_shift) & (LANES - 1), 1)
+
+
 def gather_kernel(
-    n, chunks, pupil_hbm, w_ref, wt_ref, off_ref, out_ref, pupil_ref, wide, packed, send_sem, recv_sem, own_sem
+    n, chunks, reach, pupil_hbm, w_ref, wt_ref, off_ref, out_ref,
+    pupil, wide, lined, packed, send_sem, recv_sem, own_sem,
 ):
-    load = pltpu.make_async_copy(pupil_hbm, pupil_ref, own_sem)
+    load = pltpu.make_async_copy(pupil_hbm, pupil, own_sem)
     load.start()
     me = lax.axis_index("col")
-    quarter = n // 4
-    core = lax.rem(me, 2)
-    far = quarter * (me // quarter)
-    near = lax.rem(me, quarter)
-    sibling = far + near + 1 - 2 * core
-    across_near = lax.rem(near + quarter // 2, quarter)
-    across = far + across_near
+    sibling = me + 1 - 2 * lax.rem(me, 2)
+    chips = n // 2
 
     def ahead(k):
-        return lax.rem(me + k * quarter, n)
+        return lax.rem(me + 2 * k, n)
 
     barrier = pltpu.get_barrier_semaphore()
-    partners = [ahead(1), ahead(2), ahead(3), across, sibling]
-    for partner in partners:
+    for partner in [ahead(k) for k in range(1, chips)] + [sibling]:
         pl.semaphore_signal(barrier, inc=1, device_id={"col": partner}, device_id_type=MESH)
 
+    half = half_rows(reach)
+    scalar_rows = half - reach
+    lane = lax.broadcasted_iota(jnp.int32, (scalar_rows, LANES), 1)
+    scalars = jnp.zeros((scalar_rows, LANES), jnp.float32)
+    place = 0
+    for scalar in (w_ref[0], wt_ref[0], off_ref[0].astype(jnp.float32)):
+        for piece in split3(jnp.full((scalar_rows, LANES), scalar, jnp.float32)):
+            scalars = jnp.where(lane == place, piece, scalars)
+            place += 1
+    lined[reach:half, :] = scalars
+    lined[half + reach :, :] = scalars
+    start = lax.shift_right_logical(off_ref[0], LANES.bit_length() - 1)
+    lane_shift = off_ref[0] & (LANES - 1)
+    lane = lax.broadcasted_iota(jnp.int32, (reach, LANES), 1)
     load.wait()
-    values = pupil_ref[...].astype(jnp.float32)
+    values = pupil[...].astype(jnp.float32)
     for part in range(2):
         for chunk in range(chunks):
             row = part * chunks + chunk
             wide[row : row + 1, :] = values[part : part + 1, chunk * LANES : (chunk + 1) * LANES]
-    lane = lax.broadcasted_iota(jnp.int32, (SCALAR_ROWS, LANES), 1)
-    scalars = jnp.zeros((SCALAR_ROWS, LANES), jnp.float32)
-    place = 0
-    for scalar in (w_ref[0], wt_ref[0], off_ref[0].astype(jnp.float32)):
-        for piece in split3(jnp.full((SCALAR_ROWS, LANES), scalar, jnp.float32)):
-            scalars = jnp.where(lane == place, piece, scalars)
-            place += 1
-    wide[2 * chunks :, :] = scalars
-    packed[...] = wide[...].astype(jnp.bfloat16)
+    lined[:reach, :] = shift_rows(wide, start, reach, lane_shift, lane)
+    lined[half : half + reach, :] = shift_rows(wide, chunks + start, reach, lane_shift, lane)
+    packed[...] = lined[...].astype(jnp.bfloat16)
 
     own = pltpu.make_async_copy(packed, out_ref.at[me], own_sem)
     own.start()
-    pl.semaphore_wait(barrier, len(partners))
+    pl.semaphore_wait(barrier, chips)
 
     def send(source, slot, index, partner):
         copy = pltpu.make_async_remote_copy(
@@ -121,41 +135,36 @@
         copy.start()
         return copy
 
-    copies = {k: send(packed, me, k, ahead(k)) for k in (2, 1, 3)}
-    copies[4] = send(packed, me, 4, across)
-    copies[8] = send(packed, me, 8, sibling)
-    for k in (1, 3, 2):
+    copies = {k: send(packed, me, k, ahead(k)) for k in range(1, chips)}
+    copies[chips] = send(packed, me, chips, sibling)
+    for k in ORDER:
         copies[k].wait_recv()
-        slot = lax.rem(me + (4 - k) * quarter, n)
-        copies[4 + k] = send(out_ref.at[slot], slot, 4 + k, across)
-        copies[8 + k] = send(out_ref.at[slot], slot, 8 + k, sibling)
-    for k in (0, 1, 3, 2):
-        copies[4 + k].wait_recv()
-        slot = lax.rem(far + (4 - k) * quarter, n) + across_near
-        copies[12 + k] = send(out_ref.at[slot], slot, 12 + k, sibling)
+        slot = ahead(chips - k)
+        copies[chips + k] = send(out_ref.at[slot], slot, chips + k, sibling)
     own.wait()
-    for k in range(8):
-        copies[8 + k].wait_recv()
-    for k in range(1, 16):
+    for k in range(chips):
+        copies[chips + k].wait_recv()
+    for k in range(1, n):
         copies[k].wait_send()
 
 
-def gathered_pupils(n, pupils, weights, weight_tangent, offsets):
+def gathered_pupils(n, reach, pupils, weights, weight_tangent, offsets):
     grid_size = pupils.shape[2]
     chunks = grid_size // LANES
-    rows = 2 * chunks + SCALAR_ROWS
+    rows = 2 * half_rows(reach)
     smem = pl.BlockSpec(memory_space=pltpu.SMEM)
     return pl.pallas_call(
-        functools.partial(gather_kernel, n, chunks),
+        functools.partial(gather_kernel, n, chunks, reach),
         out_shape=jax.ShapeDtypeStruct((n, rows, LANES), jnp.bfloat16),
         in_specs=[pl.BlockSpec(memory_space=pltpu.HBM), smem, smem, smem],
         out_specs=pl.BlockSpec(memory_space=pltpu.HBM),
         scratch_shapes=[
             pltpu.VMEM((2, grid_size), jnp.bfloat16),
+            pltpu.VMEM((2 * chunks, LANES), jnp.float32),
             pltpu.VMEM((rows, LANES), jnp.float32),
             pltpu.VMEM((rows, LANES), jnp.bfloat16),
-            pltpu.SemaphoreType.DMA((16,)),
-            pltpu.SemaphoreType.DMA((16,)),
+            pltpu.SemaphoreType.DMA((n,)),
+            pltpu.SemaphoreType.DMA((n,)),
             pltpu.SemaphoreType.DMA,
         ],
         compiler_params=pltpu.CompilerParams(collective_id=0, has_side_effects=True),
@@ -163,20 +172,10 @@
     )(pupils.reshape(2, grid_size), weights, weight_tangent, offsets)
 
 
-def rounded(value):
-    return value.astype(jnp.bfloat16).astype(jnp.float32)
-
-
-def shift_rows(source, start, reach, lane_shift, lane):
-    lower = source[pl.ds(start, reach), :]
-    upper = source[pl.ds(start + 1, reach), :]
-    return pltpu.roll(jnp.where(lane >= lane_shift, lower, upper), lax.rem(LANES - lane_shift, LANES), 1)
-
-
 def block_kernel(
     sources, chunks, reach, tile, width,
     row_hbm, col_hbm, all_hbm, phase_hbm, out_ref,
-    rows, cols, everything, phase, wide, shifted, factors, table, picked, right, sems,
+    rows, cols, everything, phase, shifted, factors, table, picked, right, sems,
 ):
     depth = 4 * sources
 
@@ -202,24 +201,21 @@
         copies[0].wait()
         copies[1].wait()
         lane = lax.broadcasted_iota(jnp.int32, (reach, LANES), 1)
-        offsets = []
+        half = half_rows(reach)
         for s in range(sources):
-            scalars = everything[s, 2 * chunks : 2 * chunks + SCALAR_ROWS, :].astype(jnp.float32)[:1, :]
+            spread = pl.ds(s, reach, stride=sources)
+            real = everything[s, :half, :].astype(jnp.float32)
+            shifted[0, spread, :] = real[:reach, :]
+            shifted[1, spread, :] = everything[s, half:, :].astype(jnp.float32)[:reach, :]
+            scalars = real[reach : reach + 1, :]
             one, two, three = (
                 scalars[:, i : i + 1] + scalars[:, i + 1 : i + 2] + scalars[:, i + 2 : i + 3] for i in (0, 3, 6)
             )
             factors[s : s + 1, :] = jnp.broadcast_to(one, (1, LANES))
             factors[sources + s : sources + s + 1, :] = jnp.broadcast_to(two, (1, LANES))
-            offsets.append(three[0, 0].astype(jnp.int32))
-        for s in range(sources):
-            own = wide.at[s % 2]
-            own[...] = everything[s, : 2 * chunks, :].astype(jnp.float32)
-            start = offsets[s] // LANES
-            lane_shift = lax.rem(offsets[s], LANES)
-            spread = pl.ds(s, reach, stride=sources)
-            shifted[0, spread, :] = shift_rows(own, start, reach, lane_shift, lane)
-            shifted[1, spread, :] = shift_rows(own, chunks + start, reach, lane_shift, lane)
-            shifted[2, spread, :] = shift_rows(phase, start, reach, lane_shift, lane)
+            offset = three[0, 0].astype(jnp.int32)
+            start = lax.shift_right_logical(offset, LANES.bit_length() - 1)
+            shifted[2, spread, :] = shift_rows(phase, start, reach, offset & (LANES - 1), lane)
         weight = factors[:sources, :]
         tangent = factors[sources:, :]
 
@@ -240,10 +236,10 @@
                 ],
                 axis=0,
             )
-            table[pl.ds(pl.multiple_of(chunk * LANES, LANES), LANES), :] = rounded(block).T
+            table[pl.ds(pl.multiple_of(chunk * LANES, LANES), LANES), :] = block.astype(jnp.bfloat16).T.astype(jnp.float32)
             return carry
 
-        lax.fori_loop(0, reach, one_chunk, 0, unroll=2)
+        lax.fori_loop(0, reach, one_chunk, 0, unroll=8)
 
         copies[2].wait()
         copies[3].wait()
@@ -270,7 +266,7 @@
 def block_row(sources, reach, everything, phase_tangent, row_support, col_support):
     chunks = phase_tangent.shape[0] // LANES
     rows, width = row_support.shape[0], col_support.shape[0] // sources
-    tile = 256
+    tile = TILE
     return pl.pallas_call(
         functools.partial(block_kernel, sources, chunks, reach, tile, width),
         out_shape=jax.ShapeDtypeStruct((2, rows, width), jnp.float32),
@@ -282,7 +278,6 @@
             pltpu.SMEM(col_support.shape, jnp.int32),
             pltpu.VMEM(everything.shape, jnp.bfloat16),
             pltpu.VMEM((chunks, LANES), jnp.float32),
-            pltpu.VMEM((2, 2 * chunks, LANES), jnp.float32),
             pltpu.VMEM((3, reach * sources, LANES), jnp.float32),
             pltpu.VMEM((2 * sources, LANES), jnp.float32),
             pltpu.VMEM((reach * LANES, LANES), jnp.float32),
@@ -290,7 +285,6 @@
             pltpu.VMEM((2 * width, LANES), jnp.bfloat16),
             pltpu.SemaphoreType.DMA((4,)),
         ],
-        compiler_params=pltpu.CompilerParams(vmem_limit_bytes=48 * 1024 * 1024),
         name="block_row",
     )(row_support, col_support, everything, phase_tangent.reshape(chunks, LANES))
 
@@ -303,13 +297,13 @@
     fits = (
         PARTS * n == LANES
         and grid_size % (6 * LANES) == 0
-        and rows % 256 == 0
+        and rows % TILE == 0
         and width % LANES == 0
         and grid_size * LANES * 4 <= TABLE_LIMIT_BYTES
     )
     if not fits:
         return exchanged(pupils, phase_tangent, weights, weight_tangent, offsets, row_support, col_support)
-    everything = gathered_pupils(n, pupils, weights, weight_tangent, offsets)
+    everything = gathered_pupils(n, reach, pupils, weights, weight_tangent, offsets)
     return block_row(n, reach, everything, phase_tangent, row_support, col_support)
 
 

time: 28.7 us -> 21 us (0.73)
  Pallas kernels: 23.1 us -> 18.8 us
  local copies, waits for them, and re-layouts: 3.16 us -> 0 us
    unnamed x8 -> x0, local copies, waits for them, and re-layouts: 3.16 us -> none
    pallas_call x1, Pallas kernels: 9.18 us -> 6.89 us  [block_row(): pl.pallas_call(functools.partial(block_kernel, sources, chunks, reach, ti...]
    pallas_call x1, Pallas kernels: 14 us -> 12 us  [gathered_pupils(): pl.pallas_call(functools.partial(gather_kernel, n, chunks, reach), out_sh...]
where the time goes in v3:
time: 21 us; the launch traced here: 20.8 us
  Pallas kernels  18.8 us (90%)
  between operations  1.95 us (9%)
    pallas_call x1, Pallas kernels, gathered_pupils(): pl.pallas_call(functools.partial(gather_kernel, n, chunks, reach), out_sh...  12 us
    pallas_call x1, Pallas kernels, block_row(): pl.pallas_call(functools.partial(block_kernel, sources, chunks, reach, ti...  6.89 us

profile of v3, /device:TPU:0, one launch (start us, length us, event | category | flops | bytes accessed | tf_op | source)
XLA Modules:
  0.0 20.8 jit_solution(17461913039032130833)
XLA Ops:
  1.9 12.0 %gather_pupils.1.all_hbm = bf16[16,96,128]{2,1,0:T(8,128)(2,1)} custom-call(bf16[2,6144]{1,0:T(2,128)(2,1)} %bitcast.3, f32[1]{0:T(128)S(6)} %copy.8.w_ref, f32[1]{0:T(128)S(6)} %copy.9.wt_ref, s32[1]{0:T(128)S(6)} %copy.10.off_ref), custom_call_target="tpu_custom_call" | custom-call | tf_op jit(solution)/shard_map/gather_pupils/pallas_call | solution.py:156
  13.9 6.9 %block_row.1 = f32[2,2048,256]{2,1,0:T(8,128)} custom-call(s32[2048]{0:T(1024)} %row_hbm.1, s32[4096]{0:T(1024)} %col_hbm.1, bf16[16,96,128]{2,1,0:T(8,128)(2,1)} %gather_pupils.1.all_hbm, f32[48,128]{1,0:T(8,128)} %bitcast.2), custom_call_target="tpu_custom_call" | custom-call | tf_op jit(solution)/shard_map/block_row/pallas_call | solution.py:270

commit v4 on v3

--- a/solution.py
+++ b/solution.py
@@ -9,8 +9,8 @@
 
 LANES = 128
 PARTS = 8
-PICKS = 64
-TILE = 512
+PICKS = 256
+TILE = 1024
 ORDER = (1, 7, 2, 6, 3, 5, 4)
 TABLE_LIMIT_BYTES = 8 * 1024 * 1024
 MESH = pl.DeviceIdType.MESH
@@ -239,7 +239,7 @@
             table[pl.ds(pl.multiple_of(chunk * LANES, LANES), LANES), :] = block.astype(jnp.bfloat16).T.astype(jnp.float32)
             return carry
 
-        lax.fori_loop(0, reach, one_chunk, 0, unroll=8)
+        lax.fori_loop(0, reach, one_chunk, 0, unroll=20)
 
         copies[2].wait()
         copies[3].wait()

time: 21 us -> 20.5 us (0.976)
  Pallas kernels: 18.8 us -> 18.4 us
    pallas_call x1, Pallas kernels: 6.89 us -> 6.43 us  [block_row(): pl.pallas_call(functools.partial(block_kernel, sources, chunks, reach, ti...]
where the time goes in v4:
time: 20.5 us; the launch traced here: 20.3 us
  Pallas kernels  18.4 us (90%)
  between operations  1.95 us (10%)
    pallas_call x1, Pallas kernels, gathered_pupils(): pl.pallas_call(functools.partial(gather_kernel, n, chunks, reach), out_sh...  12 us
    pallas_call x1, Pallas kernels, block_row(): pl.pallas_call(functools.partial(block_kernel, sources, chunks, reach, ti...  6.43 us

profile of v4, /device:TPU:0, one launch (start us, length us, event | category | flops | bytes accessed | tf_op | source)
XLA Modules:
  0.0 20.3 jit_solution(13059103402615739802)
XLA Ops:
  1.9 12.0 %gather_pupils.1.all_hbm = bf16[16,96,128]{2,1,0:T(8,128)(2,1)} custom-call(bf16[2,6144]{1,0:T(2,128)(2,1)} %bitcast.3, f32[1]{0:T(128)S(6)} %copy.8.w_ref, f32[1]{0:T(128)S(6)} %copy.9.wt_ref, s32[1]{0:T(128)S(6)} %copy.10.off_ref), custom_call_target="tpu_custom_call" | custom-call | tf_op jit(solution)/shard_map/gather_pupils/pallas_call | solution.py:156
  13.9 6.4 %block_row.1 = f32[2,2048,256]{2,1,0:T(8,128)} custom-call(s32[2048]{0:T(1024)} %row_hbm.1, s32[4096]{0:T(1024)} %col_hbm.1, bf16[16,96,128]{2,1,0:T(8,128)(2,1)} %gather_pupils.1.all_hbm, f32[48,128]{1,0:T(8,128)} %bitcast.2), custom_call_target="tpu_custom_call" | custom-call | tf_op jit(solution)/shard_map/block_row/pallas_call | solution.py:270
